TPU v7x, 128 devices: a whole 4x4x4 slice. The times are simulated.
128 devices in a mesh: src: 8 (over x, z_lo), shot: 16 (over z_hi, y, core).
Axes of the slice: x: 4, y: 4, z: 4 (z_hi: 2, z_lo: 2; z = z_hi * 2 + z_lo), core: 2. Of those that a mesh axis runs over, the one named last changes fastest.
Arguments:
- traces: bfloat16 [1024, 1024, 512], P('shot', 'src'), may hold values from -6 to 6
- frequency_index_list: int32 [128], replicated, may hold values from 1 to 255, as said below
- band: int32 [8, 3], replicated, may hold values 0 or 1
Outputs:
- multiples: bfloat16 [1024, 1024, 512], P('shot', 'src')
Inputs may be any that keep to these rules, and one draw needn't show every extreme that they name: `frequency_index_list`: all values differ; 1 and 255 are always among them.
All inputs are finite; a program needn't handle non-finite values.
Results may differ from a plain program's by a relative error of at most 0.0076.
Values may be sent and summed in bfloat16 or wider, within the bound.
No kernel may reach another device: no remote copies, remote signals or barrier semaphores. Data moves between devices by JAX's collectives and lax.ppermute only.
A program may use at most 128 MiB of HBM per device.

v0:
```python
import math

import jax
import jax.numpy as jnp
from jax import lax
from jax.sharding import PartitionSpec as P

NG = 1024
BS = 128


def padded(x, sides, width):
    for axis, dim in sides:
        devices, length = (lax.axis_size(axis), x.shape[dim])
        up = [(i, (i + 1) % devices) for i in range(devices - 1)]
        down = [(j, i) for i, j in up]
        last = lax.slice_in_dim(x, length - width, length, axis=dim)
        initial = lax.slice_in_dim(x, 0, width, axis=dim)
        before = lax.ppermute(last, axis, up)
        after = lax.ppermute(initial, axis, down)
        x = jnp.concatenate([before, x, after], axis=dim)
    return x


def tables(frequency_index_list, steps_count):
    steps = jnp.arange(steps_count, dtype=jnp.int32)
    phase = steps[:, None] * frequency_index_list[None, :] % steps_count
    angle = phase.astype(jnp.float32) * (2.0 * math.pi / steps_count)
    return jnp.concatenate([jnp.cos(angle), -jnp.sin(angle)], 1).astype(jnp.bfloat16)


def aperture_rows(band, nrows, column_begin, ncols):
    blocks = band.shape[0]
    row_index = jnp.arange(nrows, dtype=jnp.int32)
    row_segment = row_index // BS
    col_block = (column_begin + jnp.arange(ncols, dtype=jnp.int32)) // BS
    full_flags = (
        jnp.broadcast_to(band[:, None, :], (blocks, BS, 3)).reshape(NG, 3).astype(jnp.float32)
    )
    offset = col_block[None, :] - row_segment[:, None]
    factor = jnp.zeros((nrows, ncols), jnp.float32)
    for shift_val in (-1, 0, 1):
        factor = factor + jnp.where(
            offset == shift_val,
            full_flags[:, shift_val + 1 : shift_val + 2],
            jnp.zeros((), jnp.float32),
        )
    return factor


def aperture(band, column_begin, ncols):
    return aperture_rows(band, NG, column_begin, ncols)


def complex_product(left, right):

    def mult(left_operand, right_operand):
        return jnp.einsum(
            "axh,ahc->axc", left_operand, right_operand, preferred_element_type=jnp.float32
        )

    real_part = mult(left[0], right[0]) - mult(left[1], right[1])
    imaginary_component = mult(left[0], right[1]) + mult(left[1], right[0])
    return jnp.stack([real_part, imaginary_component])


def per_device(traces, frequency_index_list, band):
    steps_count = traces.shape[2]
    kept = frequency_index_list.shape[0]
    shot_rows = traces.shape[0]
    columns = traces.shape[1]
    table = tables(frequency_index_list, steps_count)
    spectra = lax.dot_general(
        table, traces, (((0,), (2,)), ((), ())), preferred_element_type=jnp.float32
    )
    spectra = (
        (spectra * steps_count ** (-0.5)).astype(jnp.bfloat16).reshape(2, kept, shot_rows, columns)
    )
    local = lax.all_to_all(spectra, "shot", split_axis=1, concat_axis=2, tiled=True)
    column_begin = lax.axis_index("src") * columns
    masked = (local * aperture(band, column_begin, columns)).astype(jnp.bfloat16)
    extended = padded(masked, (("src", 3),), BS)
    zero_extended = jnp.pad(masked, ((0, 0), (0, 0), (BS, BS), (0, 0)))
    right_rows = lax.dynamic_slice_in_dim(zero_extended, column_begin, columns + 2 * BS, 2)
    total = complex_product(extended, right_rows)
    product = (total * NG ** (-0.5)).astype(jnp.bfloat16)
    back = lax.all_to_all(product, "shot", split_axis=2, concat_axis=1, tiled=True)
    flat = back.reshape(2 * kept, shot_rows, columns)
    result = lax.dot_general(
        flat, table, (((0,), (1,)), ((), ())), preferred_element_type=jnp.float32
    )
    return (result * (2.0 * steps_count ** (-0.5))).astype(jnp.bfloat16)


def solution(mesh):
    placed = (P("shot", "src", None), P(), P())
    return jax.shard_map(
        per_device, mesh=mesh, in_specs=placed, out_specs=P("shot", "src", None), check_vma=False
    )
```

profile of v0, /device:TPU:1, one launch (start us, length us, event | category | flops | bytes accessed | tf_op | source)
XLA Modules:
  0.0 366.4 jit_solution(8571652972368467831)
XLA Ops:
  0.0 1.9 cosine_convert_fusion
  1.9 9.0 %multiply_convert_fusion.1 = bf16[256,64,128]{2,0,1:T(8,128)(2,1)S(1)} fusion(bf16[64,128,512]{2,1,0:T(8,128)(2,1)} %param.3, bf16[512,128]{0,1:T(8,128)(2,1)S(1)} %get-tuple-element.9, bf16[512,128]{0,1:T(8,128)(2,1)S(1)} %get-tuple-element.8), kind=kOutput, calls=%fused_computation.6 | convolution fusion | flops 2152202240 | bytes 12845056 | tf_op jit(solution)/shard_map/dot_general | solution.py:73
  10.9 6.3 %copy.17 = bf16[2,128,64,128]{3,0,2,1:T(2,128)(2,1)} copy(bf16[2,128,64,128]{3,1,0,2:T(8,128)(2,1)S(1)} %bitcast.55) | data formatting | bytes 8388608 | tf_op jit(solution)/shard_map/reshape | solution.py:77
  17.2 0.0 copy-start
  17.3 9.4 %all-to-all-start = ((bf16[2,128,64,128]{3,0,2,1:T(2,128)(2,1)}), bf16[2,128,64,128]{3,0,2,1:T(2,128)(2,1)}, u32[]{:S(2)}, u32[]{:S(2)}) async-start(bf16[2,128,64,128]{3,0,2,1:T(2,128)(2,1)} %copy.17), calls=%async_computation | async-start | bytes 8388608 | tf_op jit(solution)/shard_map/all_to_all | solution.py:79
  26.7 0.0 copy-done
  26.7 0.1 broadcast_bitcast_fusion
  26.8 0.6 select_add_fusion
  27.4 55.2 %all-to-all-done = bf16[2,128,64,128]{3,0,2,1:T(2,128)(2,1)} async-done(((bf16[2,128,64,128]{3,0,2,1:T(2,128)(2,1)}), bf16[2,128,64,128]{3,0,2,1:T(2,128)(2,1)}, u32[]{:S(2)}, u32[]{:S(2)}) %all-to-all-start) | async-done | bytes 4194336 | tf_op jit(solution)/shard_map/all_to_all | solution.py:79
  82.6 3.2 copy.18
  85.8 3.0 fusion.1
  88.8 1.3 collective-permute-start.1
  90.1 6.0 %collective-permute-start = (bf16[2,8,1024,128]{3,2,1,0:T(8,128)(2,1)}, bf16[2,8,1024,128]{3,2,1,0:T(8,128)(2,1)}, u32[]{:S(2)}, u32[]{:S(2)}) collective-permute-start(bf16[2,8,1024,128]{3,2,1,0:T(8,128)(2,1)} %fusion.1), channel_id=1, source_target_pairs={{0,16},{16,32},{32,48},{48,64},{64,80},{80,96},{96,112},{1,17},{17... | collective-permute-start | bytes 12582920 | tf_op jit(solution)/shard_map/ppermute | solution.py:19
  96.1 86.5 %collective-permute-done.1 = bf16[2,8,1024,128]{3,2,1,0:T(8,128)(2,1)} collective-permute-done((bf16[2,8,1024,128]{3,2,1,0:T(8,128)(2,1)}, bf16[2,8,1024,128]{3,2,1,0:T(8,128)(2,1)}, u32[]{:S(2)}, u32[]{:S(2)}) %collective-permute-start.1) | collective-permute-done | bytes 4194336 | tf_op jit(solution)/shard_map/ppermute | solution.py:20
  182.6 90.3 %collective-permute-done = bf16[2,8,1024,128]{3,2,1,0:T(8,128)(2,1)} collective-permute-done((bf16[2,8,1024,128]{3,2,1,0:T(8,128)(2,1)}, bf16[2,8,1024,128]{3,2,1,0:T(8,128)(2,1)}, u32[]{:S(2)}, u32[]{:S(2)}) %collective-permute-start) | collective-permute-done | bytes 4194336 | tf_op jit(solution)/shard_map/ppermute | solution.py:19
  272.8 6.4 %pad_maximum_fusion = bf16[2,8,1024,384]{3,2,1,0:T(8,128)(2,1)S(1)} fusion(bf16[2,8,1024,128]{3,2,1,0:T(8,128)(2,1)} %collective-permute-done.1, bf16[2,8,1024,128]{3,2,1,0:T(8,128)(2,1)} %fusion.1, bf16[2,8,1024,128]{3,2,1,0:T(8,128)(2,1)} %collective-permute-done), kind=kLoop, calls=%fused_computation.1 | loop fusion | flops 37748736 | bytes 25165824 | tf_op jit(solution)/shard_map/concatenate | solution.py:21
  279.3 2.9 fusion.4
  282.2 2.9 fusion.5
  285.0 2.9 add_bitcast_fusion
  287.9 2.9 subtract_bitcast_fusion
  290.8 0.8 fusion
  291.6 2.7 copy.19
  294.3 57.6 %all_to_all.24 = bf16[2,8,1024,128]{3,1,0,2:T(8,128)(2,1)S(1)} all-to-all(bf16[2,8,1024,128]{3,1,0,2:T(8,128)(2,1)S(1)} %copy.19), channel_id=1, replica_groups=mesh['src'=8,'shot'=16] {'shot'}, dimensions={2} | all-to-all | bytes 8388608 | tf_op jit(solution)/shard_map/all_to_all | solution.py:87
  351.9 1.1 copy.21
  353.0 13.4 %multiply_convert_fusion = bf16[64,128,512]{2,1,0:T(8,128)(2,1)} fusion(bf16[256,64,128]{2,1,0:T(8,128)(2,1)S(1)} %bitcast.53, bf16[512,128]{0,1:T(8,128)(2,1)S(1)} %get-tuple-element.9, bf16[512,128]{0,1:T(8,128)(2,1)S(1)} %get-tuple-element.8), kind=kOutput, calls=%fused_computation | convolution fusion | flops 2156396544 | bytes 12845056 | tf_op jit(solution)/shard_map/dot_general | solution.py:89
  (5 shorter events, 0.0 us)
Async XLA Ops:
  17.2 9.4 %copy-start = (s32[8,3]{0,1:T(4,128)S(1)}, s32[8,3]{0,1:T(4,128)}, u32[]{:S(2)}) copy-start(s32[8,3]{0,1:T(4,128)} %param.5) | copy-start | bytes 292
  17.3 65.3 %all-to-all-start = ((bf16[2,128,64,128]{3,0,2,1:T(2,128)(2,1)}), bf16[2,128,64,128]{3,0,2,1:T(2,128)(2,1)}, u32[]{:S(2)}, u32[]{:S(2)}) async-start(bf16[2,128,64,128]{3,0,2,1:T(2,128)(2,1)} %copy.17), calls=%async_computation | async-start | bytes 8388608 | tf_op jit(solution)/shard_map/all_to_all | solution.py:79
  88.8 93.7 %collective-permute-start.1 = (bf16[2,8,1024,128]{3,2,1,0:T(8,128)(2,1)}, bf16[2,8,1024,128]{3,2,1,0:T(8,128)(2,1)}, u32[]{:S(2)}, u32[]{:S(2)}) collective-permute-start(bf16[2,8,1024,128]{3,2,1,0:T(8,128)(2,1)} %fusion.1), channel_id=1, source_target_pairs={{16,0},{32,16},{48,32},{64,48},{80,64},{96,80},{112,96},{17,1},{33... | collective-permute-start | bytes 12582920 | tf_op jit(solution)/shard_map/ppermute | solution.py:20
  90.1 182.7 %collective-permute-start = (bf16[2,8,1024,128]{3,2,1,0:T(8,128)(2,1)}, bf16[2,8,1024,128]{3,2,1,0:T(8,128)(2,1)}, u32[]{:S(2)}, u32[]{:S(2)}) collective-permute-start(bf16[2,8,1024,128]{3,2,1,0:T(8,128)(2,1)} %fusion.1), channel_id=1, source_target_pairs={{0,16},{16,32},{32,48},{48,64},{64,80},{80,96},{96,112},{1,17},{17... | collective-permute-start | bytes 12582920 | tf_op jit(solution)/shard_map/ppermute | solution.py:19
where the time goes:
time: 367 us; the launch traced here: 366 us
  waiting for transfers between devices  232 us (63%)
  blocking collectives  57.6 us (16%)
  matrix products  33.9 us (9%)
  starting transfers between devices  16.7 us (5%)
  local copies, waits for them, and re-layouts  13.4 us (4%)
  other arithmetic  12.7 us (3%)
    ppermute x1, waiting for transfers between devices, padded(): before = lax.ppermute(last, axis, up)  90.3 us
    ppermute x1, waiting for transfers between devices, padded(): after = lax.ppermute(initial, axis, down)  86.5 us
    all_to_all x1, blocking collectives, per_device(): lax.all_to_all(product, 'shot', split_axis=2, concat_axis=1, tiled=True)  57.6 us
    all_to_all x1, waiting for transfers between devices, per_device(): lax.all_to_all(spectra, 'shot', split_axis=1, concat_axis=2, tiled=True)  55.2 us
    dot_general x1, matrix products, per_device(): lax.dot_general(flat, table, (((0,), (1,)), ((), ())), preferred_element_...  13.4 us
    dot_general x4, matrix products, mult(): jnp.einsum('axh,ahc->axc', left_operand, right_operand, preferred_element...  11.5 us
    all_to_all x1, starting transfers between devices, per_device(): lax.all_to_all(spectra, 'shot', split_axis=1, concat_axis=2, tiled=True)  9.43 us
    dot_general x1, matrix products, per_device(): lax.dot_general(table, traces, (((0,), (2,)), ((), ())), preferred_elemen...  9.01 us
  transfers between devices with their start and end apart: 3, of which 3 were waited for; matrix products, arithmetic and copies ran while one was open for 0% of the time, Pallas kernels for 0%

commit v1 on v0

v1 whole, which is shorter than its diff:
```python
import math

import jax
import jax.numpy as jnp
from jax import lax
from jax.experimental import pallas as pl
from jax.experimental.pallas import tpu as pltpu
from jax.sharding import PartitionSpec as P

AXES = ("src", "shot")
ROWS = 16
VMEM = 56 * 1024 * 1024


def spectral_table(frequency_index_list, steps_count):
    steps = jnp.arange(steps_count, dtype=jnp.int32)
    phase = frequency_index_list[:, None] * steps[None, :] % steps_count
    angle = phase.astype(jnp.float32) * (2.0 * math.pi / steps_count)
    return jnp.concatenate([jnp.cos(angle), -jnp.sin(angle)], 0).astype(jnp.bfloat16)


def forward_kernel(scale, table_ref, traces_ref, out_ref, total_ref):
    rows, columns, steps = traces_ref.shape
    kept = out_ref.shape[0]
    table = table_ref[...]
    for pair in range(rows // 2):
        x = traces_ref[pl.ds(2 * pair, 2)].reshape(2 * columns, steps)
        y = lax.dot_general(
            table, x, (((1,), (1,)), ((), ())), preferred_element_type=jnp.float32
        ) * scale
        for h in range(2):
            total_ref[pl.ds(2 * pair + h, 2 * kept, stride=rows), :] = y[:, h * columns : (h + 1) * columns]
    for c in range(2):
        part = total_ref[pl.ds(c * kept * rows, kept * rows), :]
        out_ref[:, c] = part.reshape(kept, rows, columns).astype(out_ref.dtype)


def forward(table, traces):
    shots, columns, steps = traces.shape
    kept = table.shape[0] // 2
    return pl.pallas_call(
        lambda *refs: forward_kernel(steps ** (-0.5), *refs),
        out_shape=jax.ShapeDtypeStruct((kept, 2, shots, columns), jnp.bfloat16),
        grid=(shots // ROWS,),
        in_specs=[
            pl.BlockSpec(table.shape, lambda g: (0, 0)),
            pl.BlockSpec((ROWS, columns, steps), lambda g: (g, 0, 0)),
        ],
        out_specs=pl.BlockSpec((kept, 2, ROWS, columns), lambda g: (0, 0, g, 0)),
        scratch_shapes=[pltpu.VMEM((2 * kept * ROWS, columns), jnp.float32)],
        compiler_params=pltpu.CompilerParams(vmem_limit_bytes=VMEM),
        name="forward",
    )(table, traces)


def product_kernel(blocks, size, scale, band_ref, in_ref, out_ref, left_ref, total_ref):
    per = size // in_ref.shape[2]

    def near(k, reach):
        return range(max(0, k - reach), min(blocks, k + reach + 1))

    for k in range(blocks):
        for b in near(k, 1):
            flag = band_ref[b, k - b + 1].astype(jnp.float32)
            for c in range(2):
                x = in_ref[pl.ds((k * blocks + b) * per, per), c].reshape(size, size)
                left_ref[k, pl.ds(b * size, size), pl.ds(c * size, size)] = (
                    x.astype(jnp.float32) * flag
                ).astype(jnp.bfloat16)
    for col in range(blocks):
        total_ref[...] = jnp.zeros_like(total_ref)
        for k in near(col, 1):
            rows = near(k, 1)
            x = left_ref[col, pl.ds(k * size, size), :]
            turned = jnp.concatenate([-x[:, size:], x[:, :size]], axis=1)
            right = jnp.concatenate([x, turned], axis=0)
            left = left_ref[k, pl.ds(rows[0] * size, len(rows) * size), :]
            total_ref[pl.ds(rows[0] * size, len(rows) * size), :] += jnp.dot(
                left, right, preferred_element_type=jnp.float32
            )
        for b in near(col, 2):
            for c in range(2):
                y = total_ref[pl.ds(b * size, size), pl.ds(c * size, size)] * scale
                out_ref[pl.ds((col * blocks + b) * per, per), c] = y.astype(jnp.bfloat16).reshape(
                    per, size // per, size
                )


def product(band, gathered):
    sources, two, shots, columns = gathered.shape
    blocks = band.shape[0]
    grid_points = blocks * columns
    return pl.pallas_call(
        lambda *refs: product_kernel(blocks, columns, grid_points ** (-0.5), *refs),
        out_shape=jax.ShapeDtypeStruct(gathered.shape, jnp.bfloat16),
        in_specs=[
            pl.BlockSpec(memory_space=pltpu.SMEM),
            pl.BlockSpec(memory_space=pltpu.VMEM),
        ],
        out_specs=pl.BlockSpec(memory_space=pltpu.VMEM),
        scratch_shapes=[
            pltpu.VMEM((blocks, grid_points, 2 * columns), jnp.bfloat16),
            pltpu.VMEM((grid_points, 2 * columns), jnp.float32),
        ],
        compiler_params=pltpu.CompilerParams(vmem_limit_bytes=VMEM),
        name="product",
    )(band, gathered)


def inverse_kernel(scale, table_ref, near_ref, in_ref, out_ref, wide_ref):
    kept, _, rows, columns = in_ref.shape

    @pl.when(near_ref[0] == 0)
    def _():
        out_ref[...] = jnp.zeros_like(out_ref)

    @pl.when(near_ref[0] != 0)
    def _():
        for c in range(2):
            wide_ref[pl.ds(c * kept * rows, kept * rows), :] = (
                in_ref[:, c].astype(jnp.float32).reshape(kept * rows, columns)
            )
        table = table_ref[...]
        for s in range(rows):
            x = wide_ref[pl.ds(s, 2 * kept, stride=rows), :].astype(jnp.bfloat16)
            y = lax.dot_general(
                x, table, (((0,), (0,)), ((), ())), preferred_element_type=jnp.float32
            )
            out_ref[s] = (y * scale).astype(out_ref.dtype)


def inverse(table, near, spectra):
    kept, two, shots, columns = spectra.shape
    steps = table.shape[1]
    return pl.pallas_call(
        lambda *refs: inverse_kernel(2.0 * steps ** (-0.5), *refs),
        out_shape=jax.ShapeDtypeStruct((shots, columns, steps), jnp.bfloat16),
        grid=(shots // ROWS,),
        in_specs=[
            pl.BlockSpec(table.shape, lambda g: (0, 0)),
            pl.BlockSpec(memory_space=pltpu.SMEM),
            pl.BlockSpec((kept, two, ROWS, columns), lambda g: (0, 0, g, 0)),
        ],
        out_specs=pl.BlockSpec((ROWS, columns, steps), lambda g: (g, 0, 0)),
        scratch_shapes=[pltpu.VMEM((2 * kept * ROWS, columns), jnp.float32)],
        compiler_params=pltpu.CompilerParams(vmem_limit_bytes=VMEM),
        name="inverse",
    )(table, near, spectra)


def per_device(traces, frequency_index_list, band):
    shots, columns, steps = traces.shape
    kept = frequency_index_list.shape[0]
    table = spectral_table(frequency_index_list, steps)
    spectra = forward(table, traces)
    gathered = lax.all_to_all(spectra, AXES, split_axis=0, concat_axis=0, tiled=True)
    made = product(band, gathered)
    back = lax.all_to_all(made, AXES, split_axis=0, concat_axis=0, tiled=True)
    row_block = lax.axis_index("shot") * shots // columns
    near = jnp.abs(row_block - lax.axis_index("src")) <= 2
    return inverse(table, near.astype(jnp.int32).reshape(1), back)


def solution(mesh):
    placed = (P("shot", "src", None), P(), P())
    return jax.shard_map(
        per_device, mesh=mesh, in_specs=placed, out_specs=P("shot", "src", None), check_vma=False
    )
```

time: 367 us -> 149 us (0.41)
  waiting for transfers between devices: 232 us -> 104 us
  blocking collectives: 57.6 us -> 0 us
  matrix products: 33.9 us -> 0 us
  Pallas kernels: 0 us -> 23.7 us
  local copies, waits for them, and re-layouts: 13.4 us -> 0.67 us
  other arithmetic: 12.7 us -> 2.61 us
    ppermute x2 -> x0, waiting for transfers between devices: 177 us -> none  [the longest x1 90.3 us: padded(): before = lax.ppermute(last, axis, up)]
    all_to_all x1 -> x0, blocking collectives: 57.6 us -> none  [per_device(): lax.all_to_all(product, 'shot', split_axis=2, concat_axis=1, tiled=True)]
    all_to_all x1 -> x2, waiting for transfers between devices: 55.2 us -> 104 us  [the longest x1 52.6 us: per_device(): back = lax.all_to_all(made, AXES, split_axis=0, concat_axis=0, tiled=True)]
    dot_general x6 -> x0, matrix products: 33.9 us -> none  [the longest x1 13.4 us: per_device(): lax.dot_general(flat, table, (((0,), (1,)), ((), ())), preferred_element_...]
    pallas_call x0 -> x3, Pallas kernels: none -> 23.7 us  [the longest x1 9.97 us: inverse(): pl.pallas_call(lambda *refs: inverse_kernel(2.0 * steps ** (-0.5), *refs)...]
    all_to_all x1 -> x2, starting transfers between devices: 9.43 us -> 17.6 us  [the longest x1 12 us: per_device(): lax.all_to_all(spectra, AXES, split_axis=0, concat_axis=0, tiled=True)]
    ppermute x2 -> x0, starting transfers between devices: 7.25 us -> none  [the longest x1 5.97 us: padded(): before = lax.ppermute(last, axis, up)]
    reshape x1 -> x0, local copies, waits for them, and re-layouts: 6.33 us -> none  [per_device(): (spectra * steps_count ** (-0.5)).astype(jnp.bfloat16)]
  transfers between devices with their start and end apart: 3 -> 2, of which waited for: 3 -> 2; matrix products, arithmetic and copies ran while one was open for 0% -> 0% of each run, Pallas kernels for 0% -> 0%
where the time goes in v1:
time: 149 us
  waiting for transfers between devices  104 us (70%)
  Pallas kernels  23.7 us (16%)
  starting transfers between devices  17.6 us (12%)
  other arithmetic  2.61 us (2%)
    all_to_all x1, waiting for transfers between devices, per_device(): back = lax.all_to_all(made, AXES, split_axis=0, concat_axis=0, tiled=True)  52.6 us
    all_to_all x1, waiting for transfers between devices, per_device(): lax.all_to_all(spectra, AXES, split_axis=0, concat_axis=0, tiled=True)  51.8 us
    all_to_all x1, starting transfers between devices, per_device(): lax.all_to_all(spectra, AXES, split_axis=0, concat_axis=0, tiled=True)  12 us
    pallas_call x1, Pallas kernels, inverse(): pl.pallas_call(lambda *refs: inverse_kernel(2.0 * steps ** (-0.5), *refs)...  9.97 us
    pallas_call x1, Pallas kernels, forward(): pl.pallas_call(lambda *refs: forward_kernel(steps ** (-0.5), *refs), out_...  8.19 us
    all_to_all x1, starting transfers between devices, per_device(): back = lax.all_to_all(made, AXES, split_axis=0, concat_axis=0, tiled=True)  5.6 us
    pallas_call x1, Pallas kernels, product(): pl.pallas_call(lambda *refs: product_kernel(blocks, columns, grid_points...  5.5 us
  transfers between devices with their start and end apart: 2, of which 2 were waited for; matrix products, arithmetic and copies ran while one was open for 0% of the time, Pallas kernels for 0%

profile of v1, /device:TPU:1, one launch (start us, length us, event | category | flops | bytes accessed | tf_op | source)
XLA Modules:
  0.0 148.9 jit_solution(4799896450934332890)
XLA Ops:
  0.0 1.9 %cosine_convert_fusion = (bf16[128,512]{1,0:T(8,128)(2,1)S(1)}, bf16[128,512]{1,0:T(8,128)(2,1)S(1)}) fusion(s32[128]{0:T(128)} %param.4), kind=kLoop, calls=%fused_computation.8 | loop fusion | flops 1114112 | bytes 262656 | tf_op jit(solution)/shard_map/convert.1
  1.9 0.7 pad_maximum_fusion.refs_0_
  2.6 8.2 %forward.1 = bf16[128,2,64,128]{3,2,1,0:T(8,128)(2,1)} custom-call(bf16[256,512]{1,0:T(8,128)(2,1)} %pad_maximum_fusion.refs_0_, bf16[64,128,512]{2,1,0:T(8,128)(2,1)} %refs_1_.1), custom_call_target="tpu_custom_call" | custom-call | tf_op jit(solution)/shard_map/forward/pallas_call | solution.py:41
  10.8 0.0 copy-start
  10.8 12.0 %all-to-all-start = ((bf16[128,2,64,128]{3,2,1,0:T(8,128)(2,1)}), bf16[128,2,64,128]{3,2,1,0:T(8,128)(2,1)}, u32[]{:S(2)}, u32[]{:S(2)}) async-start(bf16[128,2,64,128]{3,2,1,0:T(8,128)(2,1)} %forward.1), calls=%async_computation | async-start | bytes 8388608 | tf_op jit(solution)/shard_map/all_to_all | solution.py:156
  22.8 0.0 copy-done
  22.8 0.7 copy.4.refs_0_
  23.5 51.8 %all-to-all-done.refs_1_ = bf16[128,2,64,128]{3,2,1,0:T(8,128)(2,1)} async-done(((bf16[128,2,64,128]{3,2,1,0:T(8,128)(2,1)}), bf16[128,2,64,128]{3,2,1,0:T(8,128)(2,1)}, u32[]{:S(2)}, u32[]{:S(2)}) %all-to-all-start) | async-done | bytes 4194336 | tf_op jit(solution)/shard_map/all_to_all | solution.py:156
  75.3 5.5 %product.1 = bf16[128,2,64,128]{3,2,1,0:T(8,128)(2,1)} custom-call(s32[8,3]{1,0:T(8,128)} %copy.4.refs_0_, bf16[128,2,64,128]{3,2,1,0:T(8,128)(2,1)} %all-to-all-done.refs_1_), custom_call_target="tpu_custom_call" | custom-call | tf_op jit(solution)/shard_map/product/pallas_call | solution.py:93
  80.8 5.6 %all-to-all-start.1 = ((bf16[128,2,64,128]{3,2,1,0:T(8,128)(2,1)}), bf16[128,2,64,128]{3,2,1,0:T(8,128)(2,1)}, u32[]{:S(2)}, u32[]{:S(2)}) async-start(bf16[128,2,64,128]{3,2,1,0:T(8,128)(2,1)} %product.1), calls=%async_computation.1 | async-start | bytes 8388608 | tf_op jit(solution)/shard_map/all_to_all | solution.py:158
  86.4 52.6 %all-to-all-done.1.refs_2_ = bf16[128,2,64,128]{3,2,1,0:T(8,128)(2,1)} async-done(((bf16[128,2,64,128]{3,2,1,0:T(8,128)(2,1)}), bf16[128,2,64,128]{3,2,1,0:T(8,128)(2,1)}, u32[]{:S(2)}, u32[]{:S(2)}) %all-to-all-start.1) | async-done | bytes 4194336 | tf_op jit(solution)/shard_map/all_to_all | solution.py:158
  139.0 10.0 %inverse.1 = bf16[64,128,512]{2,1,0:T(8,128)(2,1)} custom-call(bf16[256,512]{1,0:T(8,128)(2,1)} %pad_maximum_fusion.refs_0_, s32[1]{0:T(128)} %bitcast.refs_1_, bf16[128,2,64,128]{3,2,1,0:T(8,128)(2,1)} %all-to-all-done.1.refs_2_), custom_call_target="tpu_custom_call" | custom-call | tf_op jit(solution)/shard_map/inverse/pallas_call | solution.py:135
Async XLA Ops:
  10.8 12.0 %copy-start = (s32[8,3]{0,1:T(4,128)S(1)}, s32[8,3]{0,1:T(4,128)}, u32[]{:S(2)}) copy-start(s32[8,3]{0,1:T(4,128)} %param.5) | copy-start | bytes 292
  10.8 64.5 %all-to-all-start = ((bf16[128,2,64,128]{3,2,1,0:T(8,128)(2,1)}), bf16[128,2,64,128]{3,2,1,0:T(8,128)(2,1)}, u32[]{:S(2)}, u32[]{:S(2)}) async-start(bf16[128,2,64,128]{3,2,1,0:T(8,128)(2,1)} %forward.1), calls=%async_computation | async-start | bytes 8388608 | tf_op jit(solution)/shard_map/all_to_all | solution.py:156
  80.8 58.2 %all-to-all-start.1 = ((bf16[128,2,64,128]{3,2,1,0:T(8,128)(2,1)}), bf16[128,2,64,128]{3,2,1,0:T(8,128)(2,1)}, u32[]{:S(2)}, u32[]{:S(2)}) async-start(bf16[128,2,64,128]{3,2,1,0:T(8,128)(2,1)} %product.1), calls=%async_computation.1 | async-start | bytes 8388608 | tf_op jit(solution)/shard_map/all_to_all | solution.py:158

commit v2 on v1

v2 whole, which is shorter than its diff:
```python
import math

import jax
import jax.numpy as jnp
from jax import lax
from jax.experimental import pallas as pl
from jax.experimental.pallas import tpu as pltpu
from jax.sharding import PartitionSpec as P

AXES = ("src", "shot")
GROUP = 16
VMEM = 28 * 1024 * 1024
FORWARD_VMEM = 54 * 1024 * 1024


def quarter_wave(theta):
    t = theta * theta
    c, s = 0.0, 0.0
    for m in range(7, -1, -1):
        c = (-1.0) ** m / math.factorial(2 * m) + c * t
        s = (-1.0) ** m / math.factorial(2 * m + 1) + s * t
    return c, s * theta


def fill_table(frequency_ref, table_ref):
    rows, steps = table_ref.shape
    kept, quarter = rows // 2, steps // 4
    frequency = jnp.broadcast_to(frequency_ref[...].astype(jnp.float32), (kept, kept)).T
    frequency = jnp.broadcast_to(frequency[:, :1], (kept, quarter)).astype(jnp.int32)
    step = lax.broadcasted_iota(jnp.int32, (kept, quarter), 1)
    phase = (frequency * step) & (steps - 1)
    turns = phase // quarter
    c, s = quarter_wave((phase - turns * quarter).astype(jnp.float32) * (2.0 * math.pi / steps))
    for q in range(4):
        turn = (turns + frequency * q) & 3
        odd, cos_flip, sin_flip = (turn & 1) == 1, (turn == 1) | (turn == 2), turn >= 2
        cos, sin = jnp.where(odd, s, c), jnp.where(odd, c, s)
        at = pl.ds(q * quarter, quarter)
        table_ref[pl.ds(0, kept), at] = jnp.where(cos_flip, -cos, cos).astype(table_ref.dtype)
        table_ref[pl.ds(kept, kept), at] = jnp.where(sin_flip, sin, -sin).astype(table_ref.dtype)


def forward_kernel(frequency_ref, traces_ref, out_ref, table_ref):
    rows, columns, steps = traces_ref.shape
    kept = out_ref.shape[0]

    @pl.when(pl.program_id(0) == 0)
    def _():
        fill_table(frequency_ref, table_ref)

    table = table_ref[...]
    made = []
    for pair in range(rows // 2):
        x = traces_ref[pl.ds(2 * pair, 2)].reshape(2 * columns, steps)
        y = lax.dot_general(
            table, x, (((1,), (1,)), ((), ())), preferred_element_type=jnp.float32
        ) * steps ** (-0.5)
        made += [y[:, :columns], y[:, columns:]]
    y = jnp.swapaxes(jnp.stack(made), 0, 1).astype(out_ref.dtype)
    for c in range(2):
        out_ref[:, c] = y[c * kept : (c + 1) * kept]


def forward(frequency_index_list, traces):
    shots, columns, steps = traces.shape
    kept = frequency_index_list.shape[0]
    return pl.pallas_call(
        forward_kernel,
        out_shape=(
            jax.ShapeDtypeStruct((kept, 2, shots, columns), jnp.bfloat16),
            jax.ShapeDtypeStruct((2 * kept, steps), jnp.bfloat16),
        ),
        grid=(shots // GROUP,),
        in_specs=[
            pl.BlockSpec((1, kept), lambda g: (0, 0)),
            pl.BlockSpec((GROUP, columns, steps), lambda g: (g, 0, 0)),
        ],
        out_specs=(
            pl.BlockSpec((kept, 2, GROUP, columns), lambda g: (0, 0, g, 0)),
            pl.BlockSpec((2 * kept, steps), lambda g: (0, 0)),
        ),
        compiler_params=pltpu.CompilerParams(vmem_limit_bytes=FORWARD_VMEM),
        name="forward",
    )(frequency_index_list.reshape(1, kept), traces)


def product_kernel(band_ref, in_ref, out_ref, left_ref, right_ref):
    blocks = band_ref.shape[1]
    size = in_ref.shape[3]
    per = size // in_ref.shape[2]
    scale = (blocks * size) ** (-0.5)

    def near(k, reach):
        return range(max(0, k - reach), min(blocks, k + reach + 1))

    for k in range(blocks):
        for b in near(k, 1):
            flag = band_ref[k - b + 1, b].astype(jnp.float32)
            for c in range(2):
                x = in_ref[pl.ds((k * blocks + b) * per, per), c].reshape(size, size)
                left_ref[k, pl.ds(b * size, size), pl.ds(c * size, size)] = (
                    x.astype(jnp.float32) * flag
                ).astype(jnp.bfloat16)
    for col in range(blocks):
        ks = near(col, 1)
        for at, k in enumerate(ks):
            x = left_ref[col, pl.ds(k * size, size), :]
            right_ref[col % 2, pl.ds(2 * at * size, size), :] = x
            right_ref[col % 2, pl.ds((2 * at + 1) * size, size), :] = jnp.concatenate(
                [-x[:, size:], x[:, :size]], axis=1
            )
        for b in near(col, 2):
            used = [k for k in ks if abs(k - b) <= 1]
            left = [left_ref[k, pl.ds(b * size, size), :] for k in used]
            right = right_ref[col % 2, pl.ds(2 * (used[0] - ks[0]) * size, 2 * len(used) * size), :]
            y = jnp.dot(
                jnp.concatenate(left, axis=1), right, preferred_element_type=jnp.float32
            ) * scale
            for c in range(2):
                out_ref[pl.ds((col * blocks + b) * per, per), c] = (
                    y[:, c * size : (c + 1) * size].astype(jnp.bfloat16).reshape(per, size // per, size)
                )


def product(band, gathered):
    sources, two, shots, columns = gathered.shape
    blocks = band.shape[0]
    return pl.pallas_call(
        product_kernel,
        out_shape=jax.ShapeDtypeStruct(gathered.shape, jnp.bfloat16),
        in_specs=[
            pl.BlockSpec(memory_space=pltpu.SMEM),
            pl.BlockSpec(memory_space=pltpu.VMEM),
        ],
        out_specs=pl.BlockSpec(memory_space=pltpu.VMEM),
        scratch_shapes=[
            pltpu.VMEM((blocks, blocks * columns, 2 * columns), jnp.bfloat16),
            pltpu.VMEM((2, 6 * columns, 2 * columns), jnp.bfloat16),
        ],
        compiler_params=pltpu.CompilerParams(vmem_limit_bytes=VMEM),
        name="product",
    )(band.T, gathered)


def inverse_kernel(table_ref, in_ref, out_ref):
    kept, _, rows, columns = in_ref.shape
    steps = table_ref.shape[1]
    row_block = lax.axis_index("shot") * (pl.num_programs(0) * rows) // columns
    near = jnp.abs(row_block - lax.axis_index("src")) <= 2

    @pl.when(jnp.logical_not(near))
    def _():
        out_ref[...] = jnp.zeros_like(out_ref)

    @pl.when(near)
    def _():
        table = table_ref[...]
        x = [jnp.swapaxes(in_ref[:, c].astype(jnp.float32), 0, 1) for c in range(2)]
        for s in range(rows):
            y = lax.dot_general(
                jnp.concatenate([x[0][s], x[1][s]], axis=0).astype(jnp.bfloat16),
                table,
                (((0,), (0,)), ((), ())),
                preferred_element_type=jnp.float32,
            )
            out_ref[s] = (y * (2.0 * steps ** (-0.5))).astype(out_ref.dtype)


def inverse(table, spectra):
    kept, two, shots, columns = spectra.shape
    steps = table.shape[1]
    return pl.pallas_call(
        inverse_kernel,
        out_shape=jax.ShapeDtypeStruct((shots, columns, steps), jnp.bfloat16),
        grid=(shots // GROUP,),
        in_specs=[
            pl.BlockSpec(table.shape, lambda g: (0, 0)),
            pl.BlockSpec((kept, two, GROUP, columns), lambda g: (0, 0, g, 0)),
        ],
        out_specs=pl.BlockSpec((GROUP, columns, steps), lambda g: (g, 0, 0)),
        compiler_params=pltpu.CompilerParams(vmem_limit_bytes=VMEM),
        name="inverse",
    )(table, spectra)


def per_device(traces, frequency_index_list, band):
    spectra, table = forward(frequency_index_list, traces)
    gathered = lax.all_to_all(spectra, AXES, split_axis=0, concat_axis=0, tiled=True)
    made = product(band, gathered)
    back = lax.all_to_all(made, AXES, split_axis=0, concat_axis=0, tiled=True)
    return inverse(table, back)


def solution(mesh):
    placed = (P("shot", "src", None), P(), P())
    return jax.shard_map(
        per_device, mesh=mesh, in_specs=placed, out_specs=P("shot", "src", None), check_vma=False
    )
```

time: 149 us -> 138 us (0.926)
  blocking collectives: 0 us -> 121 us
  waiting for transfers between devices: 104 us -> 0 us
  starting transfers between devices: 17.6 us -> 0 us
  Pallas kernels: 23.7 us -> 16.6 us
  other arithmetic: 2.61 us -> 0 us
    all_to_all x0 -> x2, blocking collectives: none -> 121 us  [the longest x1 64.3 us: per_device(): lax.all_to_all(spectra, AXES, split_axis=0, concat_axis=0, tiled=True)]
    all_to_all x2 -> x0, waiting for transfers between devices: 104 us -> none  [the longest x1 52.6 us: per_device(): back = lax.all_to_all(made, AXES, split_axis=0, concat_axis=0, tiled=True)]
    all_to_all x2 -> x0, starting transfers between devices: 17.6 us -> none  [the longest x1 12 us: per_device(): lax.all_to_all(spectra, AXES, split_axis=0, concat_axis=0, tiled=True)]
    pallas_call x3, Pallas kernels: 23.7 us -> 16.6 us  [the longest x1 8.02 us: forward(): pl.pallas_call(forward_kernel, out_shape=(jax.ShapeDtypeStruct((kept, 2,...]
    another operation x1 -> x0, other arithmetic: 1.9 us -> none
  transfers between devices with their start and end apart: 2 -> 0, of which waited for: 2 -> 0; matrix products, arithmetic and copies ran while one was open for 0% -> 0% of each run, Pallas kernels for 0% -> 0%
where the time goes in v2:
time: 138 us
  blocking collectives  121 us (88%)
  Pallas kernels  16.6 us (12%)
    all_to_all x1, blocking collectives, per_device(): lax.all_to_all(spectra, AXES, split_axis=0, concat_axis=0, tiled=True)  64.3 us
    all_to_all x1, blocking collectives, per_device(): back = lax.all_to_all(made, AXES, split_axis=0, concat_axis=0, tiled=True)  57.1 us
    pallas_call x1, Pallas kernels, forward(): pl.pallas_call(forward_kernel, out_shape=(jax.ShapeDtypeStruct((kept, 2,...  8.02 us
    pallas_call x1, Pallas kernels, inverse(): pl.pallas_call(inverse_kernel, out_shape=jax.ShapeDtypeStruct((shots, col...  6.78 us

profile of v2, /device:TPU:1, one launch (start us, length us, event | category | flops | bytes accessed | tf_op | source)
XLA Modules:
  0.0 138.1 jit_solution(17788274913910483693)
XLA Ops:
  0.0 8.0 %forward.1 = (bf16[128,2,64,128]{3,2,1,0:T(8,128)(2,1)}, bf16[256,512]{1,0:T(8,128)(2,1)}) custom-call(s32[1,128]{1,0:T(1,128)} %bitcast.3, bf16[64,128,512]{2,1,0:T(8,128)(2,1)} %traces_ref.1), custom_call_target="tpu_custom_call" | custom-call | tf_op jit(solution)/shard_map/forward/pallas_call | solution.py:67
  8.0 0.0 copy-start.1
  8.0 64.3 %all_to_all.10.in_ref = bf16[128,2,64,128]{3,2,1,0:T(8,128)(2,1)S(1)} all-to-all(bf16[128,2,64,128]{3,2,1,0:T(8,128)(2,1)} %get-tuple-element.8), channel_id=1, replica_groups=mesh['src'=8,'shot'=16] {'src','shot'}, dimensions={0} | all-to-all | bytes 8388608 | tf_op jit(solution)/shard_map/all_to_all | solution.py:188
  72.3 0.0 copy-done.1
  72.3 1.8 %product.1 = bf16[128,2,64,128]{3,2,1,0:T(8,128)(2,1)S(1)} custom-call(s32[3,8]{1,0:T(4,128)S(1)} %bitcast.2, bf16[128,2,64,128]{3,2,1,0:T(8,128)(2,1)S(1)} %all_to_all.10.in_ref), custom_call_target="tpu_custom_call" | custom-call | tf_op jit(solution)/shard_map/product/pallas_call | solution.py:128
  74.2 0.0 copy-start
  74.2 57.1 %all_to_all.11.in_ref = bf16[128,2,64,128]{3,2,1,0:T(8,128)(2,1)S(1)} all-to-all(bf16[128,2,64,128]{3,2,1,0:T(8,128)(2,1)S(1)} %product.1), channel_id=1, replica_groups=mesh['src'=8,'shot'=16] {'src','shot'}, dimensions={0} | all-to-all | bytes 8388608 | tf_op jit(solution)/shard_map/all_to_all | solution.py:190
  131.3 0.0 copy-done
  131.3 6.8 %inverse.1 = bf16[64,128,512]{2,1,0:T(8,128)(2,1)} custom-call(bf16[256,512]{1,0:T(8,128)(2,1)S(1)} %copy-done, bf16[128,2,64,128]{3,2,1,0:T(8,128)(2,1)S(1)} %all_to_all.11.in_ref), custom_call_target="tpu_custom_call" | custom-call | tf_op jit(solution)/shard_map/inverse/pallas_call | solution.py:172
Async XLA Ops:
  8.0 64.3 %copy-start.1 = (s32[8,3]{0,1:T(4,128)S(1)}, s32[8,3]{0,1:T(4,128)}, u32[]{:S(2)}) copy-start(s32[8,3]{0,1:T(4,128)} %param.5) | copy-start | bytes 292
  74.2 57.1 %copy-start = (bf16[256,512]{1,0:T(8,128)(2,1)S(1)}, bf16[256,512]{1,0:T(8,128)(2,1)}, u32[]{:S(2)}) copy-start(bf16[256,512]{1,0:T(8,128)(2,1)} %get-tuple-element.7.table_ref) | copy-start | bytes 786436

commit v3 on v2

--- a/solution.py
+++ b/solution.py
@@ -9,8 +9,8 @@
 
 AXES = ("src", "shot")
 GROUP = 16
+PART = 8
 VMEM = 28 * 1024 * 1024
-FORWARD_VMEM = 54 * 1024 * 1024
 
 
 def quarter_wave(theta):
@@ -40,25 +40,33 @@
         table_ref[pl.ds(kept, kept), at] = jnp.where(sin_flip, sin, -sin).astype(table_ref.dtype)
 
 
-def forward_kernel(frequency_ref, traces_ref, out_ref, table_ref):
-    rows, columns, steps = traces_ref.shape
+def forward_kernel(frequency_hbm, traces_ref, out_ref, table_ref, frequency_ref, held_ref, here, arrived):
+    shots, columns, steps = traces_ref.shape
     kept = out_ref.shape[0]
-
-    @pl.when(pl.program_id(0) == 0)
-    def _():
-        fill_table(frequency_ref, table_ref)
-
+    starts = range(0, shots, GROUP)
+    copies = [
+        pltpu.make_async_copy(traces_ref.at[pl.ds(s, GROUP)], held_ref.at[pl.ds(s, GROUP)], arrived.at[n])
+        for n, s in enumerate(starts)
+    ]
+    first = pltpu.make_async_copy(frequency_hbm, frequency_ref, here)
+    first.start()
+    for copy in copies:
+        copy.start()
+    first.wait()
+    fill_table(frequency_ref, table_ref)
     table = table_ref[...]
-    made = []
-    for pair in range(rows // 2):
-        x = traces_ref[pl.ds(2 * pair, 2)].reshape(2 * columns, steps)
-        y = lax.dot_general(
-            table, x, (((1,), (1,)), ((), ())), preferred_element_type=jnp.float32
-        ) * steps ** (-0.5)
-        made += [y[:, :columns], y[:, columns:]]
-    y = jnp.swapaxes(jnp.stack(made), 0, 1).astype(out_ref.dtype)
-    for c in range(2):
-        out_ref[:, c] = y[c * kept : (c + 1) * kept]
+    for start, copy in zip(starts, copies):
+        copy.wait()
+        made = []
+        for s in range(start, start + GROUP, 2):
+            x = held_ref[pl.ds(s, 2)].reshape(2 * columns, steps)
+            y = lax.dot_general(
+                table, x, (((1,), (1,)), ((), ())), preferred_element_type=jnp.float32
+            ) * steps ** (-0.5)
+            made += [y[:, :columns], y[:, columns:]]
+        y = jnp.swapaxes(jnp.stack(made), 0, 1).astype(out_ref.dtype)
+        for c in range(2):
+            out_ref[:, c, pl.ds(start, GROUP)] = y[c * kept : (c + 1) * kept]
 
 
 def forward(frequency_index_list, traces):
@@ -70,18 +78,23 @@
             jax.ShapeDtypeStruct((kept, 2, shots, columns), jnp.bfloat16),
             jax.ShapeDtypeStruct((2 * kept, steps), jnp.bfloat16),
         ),
-        grid=(shots // GROUP,),
-        in_specs=[
-            pl.BlockSpec((1, kept), lambda g: (0, 0)),
-            pl.BlockSpec((GROUP, columns, steps), lambda g: (g, 0, 0)),
-        ],
+        in_specs=[pl.BlockSpec(memory_space=pltpu.HBM)] * 2,
         out_specs=(
-            pl.BlockSpec((kept, 2, GROUP, columns), lambda g: (0, 0, g, 0)),
-            pl.BlockSpec((2 * kept, steps), lambda g: (0, 0)),
+            pl.BlockSpec(memory_space=pltpu.VMEM),
+            pl.BlockSpec(memory_space=pltpu.VMEM),
         ),
-        compiler_params=pltpu.CompilerParams(vmem_limit_bytes=FORWARD_VMEM),
+        scratch_shapes=[
+            pltpu.VMEM((1, kept), jnp.int32),
+            pltpu.VMEM(traces.shape, traces.dtype),
+            pltpu.SemaphoreType.DMA(()),
+            pltpu.SemaphoreType.DMA((shots // GROUP,)),
+        ],
+        compiler_params=pltpu.CompilerParams(vmem_limit_bytes=VMEM),
         name="forward",
-    )(frequency_index_list.reshape(1, kept), traces)
+    )(
+        pltpu.with_memory_space_constraint(frequency_index_list.reshape(1, kept), pltpu.HBM),
+        pltpu.with_memory_space_constraint(traces, pltpu.HBM),
+    )
 
 
 def product_kernel(band_ref, in_ref, out_ref, left_ref, right_ref):
@@ -142,28 +155,38 @@
     )(band.T, gathered)
 
 
-def inverse_kernel(table_ref, in_ref, out_ref):
-    kept, _, rows, columns = in_ref.shape
+def inverse_kernel(table_ref, in_ref, out_ref, held_ref, sent):
+    kept, _, shots, columns = in_ref.shape
     steps = table_ref.shape[1]
-    row_block = lax.axis_index("shot") * (pl.num_programs(0) * rows) // columns
+    row_block = lax.axis_index("shot") * shots // columns
     near = jnp.abs(row_block - lax.axis_index("src")) <= 2
+    copies = [
+        pltpu.make_async_copy(held_ref.at[pl.ds(s, PART)], out_ref.at[pl.ds(s, PART)], sent.at[n])
+        for n, s in enumerate(range(0, shots, PART))
+    ]
 
     @pl.when(jnp.logical_not(near))
     def _():
-        out_ref[...] = jnp.zeros_like(out_ref)
+        held_ref[...] = jnp.zeros_like(held_ref)
+        for copy in copies:
+            copy.start()
 
     @pl.when(near)
     def _():
         table = table_ref[...]
-        x = [jnp.swapaxes(in_ref[:, c].astype(jnp.float32), 0, 1) for c in range(2)]
-        for s in range(rows):
-            y = lax.dot_general(
-                jnp.concatenate([x[0][s], x[1][s]], axis=0).astype(jnp.bfloat16),
-                table,
-                (((0,), (0,)), ((), ())),
-                preferred_element_type=jnp.float32,
-            )
-            out_ref[s] = (y * (2.0 * steps ** (-0.5))).astype(out_ref.dtype)
+        for start in range(0, shots, GROUP):
+            x = [jnp.swapaxes(in_ref[:, c, pl.ds(start, GROUP)], 0, 1) for c in range(2)]
+            for s in range(0, GROUP, 4):
+                lines = [jnp.concatenate([x[0][n], x[1][n]], axis=0).T for n in range(s, s + 4)]
+                y = jnp.dot(
+                    jnp.concatenate(lines, axis=0), table, preferred_element_type=jnp.float32
+                ) * (2.0 * steps ** (-0.5))
+                held_ref[pl.ds(start + s, 4)] = y.astype(out_ref.dtype).reshape(4, columns, steps)
+                if (start + s + 4) % PART == 0:
+                    copies[(start + s) // PART].start()
+
+    for copy in copies:
+        copy.wait()
 
 
 def inverse(table, spectra):
@@ -172,12 +195,12 @@
     return pl.pallas_call(
         inverse_kernel,
         out_shape=jax.ShapeDtypeStruct((shots, columns, steps), jnp.bfloat16),
-        grid=(shots // GROUP,),
-        in_specs=[
-            pl.BlockSpec(table.shape, lambda g: (0, 0)),
-            pl.BlockSpec((kept, two, GROUP, columns), lambda g: (0, 0, g, 0)),
-        ],
-        out_specs=pl.BlockSpec((GROUP, columns, steps), lambda g: (g, 0, 0)),
+        in_specs=[pl.BlockSpec(memory_space=pltpu.VMEM)] * 2,
+        out_specs=pl.BlockSpec(memory_space=pltpu.HBM),
+        scratch_shapes=[
+            pltpu.VMEM((shots, columns, steps), jnp.bfloat16),
+            pltpu.SemaphoreType.DMA((shots // PART,)),
+        ],
         compiler_params=pltpu.CompilerParams(vmem_limit_bytes=VMEM),
         name="inverse",
     )(table, spectra)

time: 138 us -> 134 us (0.971)
  Pallas kernels: 16.6 us -> 13 us
    pallas_call x1, Pallas kernels: 6.78 us -> 4.34 us  [inverse(): pl.pallas_call(inverse_kernel, out_shape=jax.ShapeDtypeStruct((shots, col...]
where the time goes in v3:
time: 134 us
  blocking collectives  121 us (90%)
  Pallas kernels  13 us (10%)
    all_to_all x1, blocking collectives, per_device(): lax.all_to_all(spectra, AXES, split_axis=0, concat_axis=0, tiled=True)  64.1 us
    all_to_all x1, blocking collectives, per_device(): back = lax.all_to_all(made, AXES, split_axis=0, concat_axis=0, tiled=True)  57.1 us
    pallas_call x1, Pallas kernels, forward(): pl.pallas_call(forward_kernel, out_shape=(jax.ShapeDtypeStruct((kept, 2,...  6.81 us
    pallas_call x1, Pallas kernels, inverse(): pl.pallas_call(inverse_kernel, out_shape=jax.ShapeDtypeStruct((shots, col...  4.34 us

profile of v3, /device:TPU:1, one launch (start us, length us, event | category | flops | bytes accessed | tf_op | source)
XLA Modules:
  0.0 134.2 jit_solution(15390537748383915368)
XLA Ops:
  0.0 6.8 %forward.1 = (bf16[128,2,64,128]{3,2,1,0:T(8,128)(2,1)S(1)}, bf16[256,512]{1,0:T(8,128)(2,1)S(1)}) custom-call(s32[1,128]{1,0:T(1,128)} %bitcast.3, bf16[64,128,512]{2,1,0:T(8,128)(2,1)} %traces_ref.1), custom_call_target="tpu_custom_call" | custom-call | tf_op jit(solution)/shard_map/forward/pallas_call | solution.py:75
  6.8 0.0 copy-start
  6.8 64.1 %all_to_all.10.in_ref = bf16[128,2,64,128]{3,2,1,0:T(8,128)(2,1)S(1)} all-to-all(bf16[128,2,64,128]{3,2,1,0:T(8,128)(2,1)S(1)} %get-tuple-element.8), channel_id=1, replica_groups=mesh['src'=8,'shot'=16] {'src','shot'}, dimensions={0} | all-to-all | bytes 8388608 | tf_op jit(solution)/shard_map/all_to_all | solution.py:211
  71.0 0.0 copy-done
  71.0 1.8 %product.1 = bf16[128,2,64,128]{3,2,1,0:T(8,128)(2,1)S(1)} custom-call(s32[3,8]{1,0:T(4,128)S(1)} %bitcast.2, bf16[128,2,64,128]{3,2,1,0:T(8,128)(2,1)S(1)} %all_to_all.10.in_ref), custom_call_target="tpu_custom_call" | custom-call | tf_op jit(solution)/shard_map/product/pallas_call | solution.py:141
  72.8 57.1 %all_to_all.11.in_ref = bf16[128,2,64,128]{3,2,1,0:T(8,128)(2,1)S(1)} all-to-all(bf16[128,2,64,128]{3,2,1,0:T(8,128)(2,1)S(1)} %product.1), channel_id=1, replica_groups=mesh['src'=8,'shot'=16] {'src','shot'}, dimensions={0} | all-to-all | bytes 8388608 | tf_op jit(solution)/shard_map/all_to_all | solution.py:213
  129.9 4.3 %inverse.1 = bf16[64,128,512]{2,1,0:T(8,128)(2,1)} custom-call(bf16[256,512]{1,0:T(8,128)(2,1)S(1)} %get-tuple-element.7.table_ref, bf16[128,2,64,128]{3,2,1,0:T(8,128)(2,1)S(1)} %all_to_all.11.in_ref), custom_call_target="tpu_custom_call" | custom-call | tf_op jit(solution)/shard_map/inverse/pallas_call | solution.py:195
Async XLA Ops:
  6.8 64.1 %copy-start = (s32[8,3]{0,1:T(4,128)S(1)}, s32[8,3]{0,1:T(4,128)}, u32[]{:S(2)}) copy-start(s32[8,3]{0,1:T(4,128)} %param.5) | copy-start | bytes 292

commit v4 on v3

--- a/solution.py
+++ b/solution.py
@@ -50,9 +50,10 @@
     ]
     first = pltpu.make_async_copy(frequency_hbm, frequency_ref, here)
     first.start()
-    for copy in copies:
+    copies[0].start()
+    first.wait()
+    for copy in copies[1:]:
         copy.start()
-    first.wait()
     fill_table(frequency_ref, table_ref)
     table = table_ref[...]
     for start, copy in zip(starts, copies):

time: 134 us -> 133 us (level)
  Pallas kernels: 13 us -> 11.6 us
    pallas_call x1, Pallas kernels: 6.81 us -> 5.46 us  [forward(): pl.pallas_call(forward_kernel, out_shape=(jax.ShapeDtypeStruct((kept, 2,...]
where the time goes in v4:
time: 133 us
  blocking collectives  121 us (91%)
  Pallas kernels  11.6 us (9%)
    all_to_all x1, blocking collectives, per_device(): lax.all_to_all(spectra, AXES, split_axis=0, concat_axis=0, tiled=True)  64.1 us
    all_to_all x1, blocking collectives, per_device(): back = lax.all_to_all(made, AXES, split_axis=0, concat_axis=0, tiled=True)  57.1 us
    pallas_call x1, Pallas kernels, forward(): pl.pallas_call(forward_kernel, out_shape=(jax.ShapeDtypeStruct((kept, 2,...  5.46 us
    pallas_call x1, Pallas kernels, inverse(): pl.pallas_call(inverse_kernel, out_shape=jax.ShapeDtypeStruct((shots, col...  4.32 us

profile of v4, /device:TPU:1, one launch (start us, length us, event | category | flops | bytes accessed | tf_op | source)
XLA Modules:
  0.0 132.9 jit_solution(3902240007827785715)
XLA Ops:
  0.0 5.5 %forward.1 = (bf16[128,2,64,128]{3,2,1,0:T(8,128)(2,1)S(1)}, bf16[256,512]{1,0:T(8,128)(2,1)S(1)}) custom-call(s32[1,128]{1,0:T(1,128)} %bitcast.3, bf16[64,128,512]{2,1,0:T(8,128)(2,1)} %traces_ref.1), custom_call_target="tpu_custom_call" | custom-call | tf_op jit(solution)/shard_map/forward/pallas_call | solution.py:76
  5.5 0.0 copy-start
  5.5 64.1 %all_to_all.10.in_ref = bf16[128,2,64,128]{3,2,1,0:T(8,128)(2,1)S(1)} all-to-all(bf16[128,2,64,128]{3,2,1,0:T(8,128)(2,1)S(1)} %get-tuple-element.8), channel_id=1, replica_groups=mesh['src'=8,'shot'=16] {'src','shot'}, dimensions={0} | all-to-all | bytes 8388608 | tf_op jit(solution)/shard_map/all_to_all | solution.py:212
  69.6 0.0 copy-done
  69.6 1.8 %product.1 = bf16[128,2,64,128]{3,2,1,0:T(8,128)(2,1)S(1)} custom-call(s32[3,8]{1,0:T(4,128)S(1)} %bitcast.2, bf16[128,2,64,128]{3,2,1,0:T(8,128)(2,1)S(1)} %all_to_all.10.in_ref), custom_call_target="tpu_custom_call" | custom-call | tf_op jit(solution)/shard_map/product/pallas_call | solution.py:142
  71.4 57.1 %all_to_all.11.in_ref = bf16[128,2,64,128]{3,2,1,0:T(8,128)(2,1)S(1)} all-to-all(bf16[128,2,64,128]{3,2,1,0:T(8,128)(2,1)S(1)} %product.1), channel_id=1, replica_groups=mesh['src'=8,'shot'=16] {'src','shot'}, dimensions={0} | all-to-all | bytes 8388608 | tf_op jit(solution)/shard_map/all_to_all | solution.py:214
  128.5 4.3 %inverse.1 = bf16[64,128,512]{2,1,0:T(8,128)(2,1)} custom-call(bf16[256,512]{1,0:T(8,128)(2,1)S(1)} %get-tuple-element.7.table_ref, bf16[128,2,64,128]{3,2,1,0:T(8,128)(2,1)S(1)} %all_to_all.11.in_ref), custom_call_target="tpu_custom_call" | custom-call | tf_op jit(solution)/shard_map/inverse/pallas_call | solution.py:196
Async XLA Ops:
  5.5 64.1 %copy-start = (s32[8,3]{0,1:T(4,128)S(1)}, s32[8,3]{0,1:T(4,128)}, u32[]{:S(2)}) copy-start(s32[8,3]{0,1:T(4,128)} %param.5) | copy-start | bytes 292

commit v5 on v4

--- a/solution.py
+++ b/solution.py
@@ -9,7 +9,8 @@
 
 AXES = ("src", "shot")
 GROUP = 16
-PART = 8
+PART = 4
+CHUNKS = (16, 16, 32)
 VMEM = 28 * 1024 * 1024
 
 
@@ -43,10 +44,10 @@
 def forward_kernel(frequency_hbm, traces_ref, out_ref, table_ref, frequency_ref, held_ref, here, arrived):
     shots, columns, steps = traces_ref.shape
     kept = out_ref.shape[0]
-    starts = range(0, shots, GROUP)
+    begins = [sum(CHUNKS[:n]) for n in range(len(CHUNKS))]
     copies = [
-        pltpu.make_async_copy(traces_ref.at[pl.ds(s, GROUP)], held_ref.at[pl.ds(s, GROUP)], arrived.at[n])
-        for n, s in enumerate(starts)
+        pltpu.make_async_copy(traces_ref.at[pl.ds(s, size)], held_ref.at[pl.ds(s, size)], arrived.at[n])
+        for n, (s, size) in enumerate(zip(begins, CHUNKS))
     ]
     first = pltpu.make_async_copy(frequency_hbm, frequency_ref, here)
     first.start()
@@ -56,8 +57,9 @@
         copy.start()
     fill_table(frequency_ref, table_ref)
     table = table_ref[...]
-    for start, copy in zip(starts, copies):
-        copy.wait()
+    for start in range(0, shots, GROUP):
+        if start in begins:
+            copies[begins.index(start)].wait()
         made = []
         for s in range(start, start + GROUP, 2):
             x = held_ref[pl.ds(s, 2)].reshape(2 * columns, steps)
@@ -88,7 +90,7 @@
             pltpu.VMEM((1, kept), jnp.int32),
             pltpu.VMEM(traces.shape, traces.dtype),
             pltpu.SemaphoreType.DMA(()),
-            pltpu.SemaphoreType.DMA((shots // GROUP,)),
+            pltpu.SemaphoreType.DMA((len(CHUNKS),)),
         ],
         compiler_params=pltpu.CompilerParams(vmem_limit_bytes=VMEM),
         name="forward",

time: 133 us -> 133 us (level)
  no operation moved by 1% of the time
where the time goes in v5:
time: 133 us
  blocking collectives  121 us (91%)
  Pallas kernels  11.4 us (9%)
    all_to_all x1, blocking collectives, per_device(): lax.all_to_all(spectra, AXES, split_axis=0, concat_axis=0, tiled=True)  64.1 us
    all_to_all x1, blocking collectives, per_device(): back = lax.all_to_all(made, AXES, split_axis=0, concat_axis=0, tiled=True)  57.1 us
    pallas_call x1, Pallas kernels, forward(): pl.pallas_call(forward_kernel, out_shape=(jax.ShapeDtypeStruct((kept, 2,...  5.35 us
    pallas_call x1, Pallas kernels, inverse(): pl.pallas_call(inverse_kernel, out_shape=jax.ShapeDtypeStruct((shots, col...  4.25 us

profile of v5, /device:TPU:1, one launch (start us, length us, event | category | flops | bytes accessed | tf_op | source)
XLA Modules:
  0.0 132.7 jit_solution(6265929905585104571)
XLA Ops:
  0.0 5.4 %forward.1 = (bf16[128,2,64,128]{3,2,1,0:T(8,128)(2,1)S(1)}, bf16[256,512]{1,0:T(8,128)(2,1)S(1)}) custom-call(s32[1,128]{1,0:T(1,128)} %bitcast.3, bf16[64,128,512]{2,1,0:T(8,128)(2,1)} %traces_ref.1), custom_call_target="tpu_custom_call" | custom-call | tf_op jit(solution)/shard_map/forward/pallas_call | solution.py:78
  5.4 0.0 copy-start
  5.4 64.1 %all_to_all.10.in_ref = bf16[128,2,64,128]{3,2,1,0:T(8,128)(2,1)S(1)} all-to-all(bf16[128,2,64,128]{3,2,1,0:T(8,128)(2,1)S(1)} %get-tuple-element.8), channel_id=1, replica_groups=mesh['src'=8,'shot'=16] {'src','shot'}, dimensions={0} | all-to-all | bytes 8388608 | tf_op jit(solution)/shard_map/all_to_all | solution.py:214
  69.5 0.0 copy-done
  69.5 1.8 %product.1 = bf16[128,2,64,128]{3,2,1,0:T(8,128)(2,1)S(1)} custom-call(s32[3,8]{1,0:T(4,128)S(1)} %bitcast.2, bf16[128,2,64,128]{3,2,1,0:T(8,128)(2,1)S(1)} %all_to_all.10.in_ref), custom_call_target="tpu_custom_call" | custom-call | tf_op jit(solution)/shard_map/product/pallas_call | solution.py:144
  71.3 57.1 %all_to_all.11.in_ref = bf16[128,2,64,128]{3,2,1,0:T(8,128)(2,1)S(1)} all-to-all(bf16[128,2,64,128]{3,2,1,0:T(8,128)(2,1)S(1)} %product.1), channel_id=1, replica_groups=mesh['src'=8,'shot'=16] {'src','shot'}, dimensions={0} | all-to-all | bytes 8388608 | tf_op jit(solution)/shard_map/all_to_all | solution.py:216
  128.4 4.2 %inverse.1 = bf16[64,128,512]{2,1,0:T(8,128)(2,1)} custom-call(bf16[256,512]{1,0:T(8,128)(2,1)S(1)} %get-tuple-element.7.table_ref, bf16[128,2,64,128]{3,2,1,0:T(8,128)(2,1)S(1)} %all_to_all.11.in_ref), custom_call_target="tpu_custom_call" | custom-call | tf_op jit(solution)/shard_map/inverse/pallas_call | solution.py:198
Async XLA Ops:
  5.4 64.1 %copy-start = (s32[8,3]{0,1:T(4,128)S(1)}, s32[8,3]{0,1:T(4,128)}, u32[]{:S(2)}) copy-start(s32[8,3]{0,1:T(4,128)} %param.5) | copy-start | bytes 292

commit v6 on v5

--- a/solution.py
+++ b/solution.py
@@ -177,8 +177,15 @@
     @pl.when(near)
     def _():
         table = table_ref[...]
+
+        def turned(start):
+            return [jnp.swapaxes(in_ref[:, c, pl.ds(start, GROUP)], 0, 1) for c in range(2)]
+
+        after = turned(0)
         for start in range(0, shots, GROUP):
-            x = [jnp.swapaxes(in_ref[:, c, pl.ds(start, GROUP)], 0, 1) for c in range(2)]
+            x = after
+            if start + GROUP < shots:
+                after = turned(start + GROUP)
             for s in range(0, GROUP, 4):
                 lines = [jnp.concatenate([x[0][n], x[1][n]], axis=0).T for n in range(s, s + 4)]
                 y = jnp.dot(

time: 133 us -> 133 us (level)
  no operation moved by 1% of the time
where the time goes in v6:
time: 133 us
  blocking collectives  121 us (91%)
  Pallas kernels  11.4 us (9%)
    all_to_all x1, blocking collectives, per_device(): lax.all_to_all(spectra, AXES, split_axis=0, concat_axis=0, tiled=True)  64.1 us
    all_to_all x1, blocking collectives, per_device(): back = lax.all_to_all(made, AXES, split_axis=0, concat_axis=0, tiled=True)  57.1 us
    pallas_call x1, Pallas kernels, forward(): pl.pallas_call(forward_kernel, out_shape=(jax.ShapeDtypeStruct((kept, 2,...  5.35 us
    pallas_call x1, Pallas kernels, inverse(): pl.pallas_call(inverse_kernel, out_shape=jax.ShapeDtypeStruct((shots, col...  4.25 us

profile of v6, /device:TPU:1, one launch (start us, length us, event | category | flops | bytes accessed | tf_op | source)
XLA Modules:
  0.0 132.7 jit_solution(6265929905585104571)
XLA Ops:
  0.0 5.4 %forward.1 = (bf16[128,2,64,128]{3,2,1,0:T(8,128)(2,1)S(1)}, bf16[256,512]{1,0:T(8,128)(2,1)S(1)}) custom-call(s32[1,128]{1,0:T(1,128)} %bitcast.3, bf16[64,128,512]{2,1,0:T(8,128)(2,1)} %traces_ref.1), custom_call_target="tpu_custom_call" | custom-call | tf_op jit(solution)/shard_map/forward/pallas_call | solution.py:78
  5.4 0.0 copy-start
  5.4 64.1 %all_to_all.10.in_ref = bf16[128,2,64,128]{3,2,1,0:T(8,128)(2,1)S(1)} all-to-all(bf16[128,2,64,128]{3,2,1,0:T(8,128)(2,1)S(1)} %get-tuple-element.8), channel_id=1, replica_groups=mesh['src'=8,'shot'=16] {'src','shot'}, dimensions={0} | all-to-all | bytes 8388608 | tf_op jit(solution)/shard_map/all_to_all | solution.py:221
  69.5 0.0 copy-done
  69.5 1.8 %product.1 = bf16[128,2,64,128]{3,2,1,0:T(8,128)(2,1)S(1)} custom-call(s32[3,8]{1,0:T(4,128)S(1)} %bitcast.2, bf16[128,2,64,128]{3,2,1,0:T(8,128)(2,1)S(1)} %all_to_all.10.in_ref), custom_call_target="tpu_custom_call" | custom-call | tf_op jit(solution)/shard_map/product/pallas_call | solution.py:144
  71.3 57.1 %all_to_all.11.in_ref = bf16[128,2,64,128]{3,2,1,0:T(8,128)(2,1)S(1)} all-to-all(bf16[128,2,64,128]{3,2,1,0:T(8,128)(2,1)S(1)} %product.1), channel_id=1, replica_groups=mesh['src'=8,'shot'=16] {'src','shot'}, dimensions={0} | all-to-all | bytes 8388608 | tf_op jit(solution)/shard_map/all_to_all | solution.py:223
  128.4 4.2 %inverse.1 = bf16[64,128,512]{2,1,0:T(8,128)(2,1)} custom-call(bf16[256,512]{1,0:T(8,128)(2,1)S(1)} %get-tuple-element.7.table_ref, bf16[128,2,64,128]{3,2,1,0:T(8,128)(2,1)S(1)} %all_to_all.11.in_ref), custom_call_target="tpu_custom_call" | custom-call | tf_op jit(solution)/shard_map/inverse/pallas_call | solution.py:205
Async XLA Ops:
  5.4 64.1 %copy-start = (s32[8,3]{0,1:T(4,128)S(1)}, s32[8,3]{0,1:T(4,128)}, u32[]{:S(2)}) copy-start(s32[8,3]{0,1:T(4,128)} %param.5) | copy-start | bytes 292
